TPU v7x, 32 devices: a whole 2x2x4 slice. The times are simulated.
32 devices in a mesh: row: 4 (over y, x), col: 8 (over z, core).
Axes of the slice: x: 2, y: 2, z: 4, core: 2. Of those that a mesh axis runs over, the one named last changes fastest.
Arguments:
- amplitudes: bfloat16 [16, 768, 768], P('row', 'col'), may hold values from -6 to 6
- factors: bfloat16 [32, 768, 768], P('col', 'row'), may hold values from -0.109375 to 0.109375
- counts: int32 [4], replicated, may hold values from 1 to 4, 8 in all
- pair_index: int32 [16, 2], replicated, may hold values from 0 to 23
- occ_energy: float32 [24], replicated, may hold values from -2 to -0.5
- vir_energy: float32 [768], replicated, may hold values from 0.5 to 3
Outputs:
- new_amplitudes: bfloat16 [16, 768, 768], P('row', 'col')
Inputs may be any that keep to these rules, and one draw needn't show every extreme that they name: The counts sum to 2 times the number of owner rows. `pair_index`: entries of slots that are not live are not used.
All inputs are finite; a program needn't handle non-finite values.
Results may differ from a plain program's by a relative error of at most 0.0046.
Values may be sent and summed in bfloat16 or wider, within the bound.
A program may use at most 64 MiB of HBM per device.

v0:
```python
import jax
import jax.numpy as jnp
from jax import lax
from jax.sharding import PartitionSpec as P

WORK = 2


level_shift = 1.0


def per_device(amplitudes, factors, counts, pair_index, occ_energy, vir_energy):
    slot_count = amplitudes.shape[0]
    col_rows = amplitudes.shape[1]
    row_id = lax.axis_index("row")
    col_id = lax.axis_index("col")
    full_factors = lax.all_gather(factors, "row", axis=1, tiled=True)
    starts = jnp.cumsum(counts) - counts
    local_slots = jnp.arange(slot_count, dtype=jnp.int32)
    own_rank = starts[row_id] + local_slots
    own_live = local_slots < counts[row_id]
    everyone = lax.all_gather(amplitudes, "row", axis=0, tiled=True)
    total_slots = everyone.shape[0]
    global_ids = jnp.arange(total_slots, dtype=jnp.int32)
    owner_rows = global_ids // slot_count
    within = global_ids % slot_count
    global_rank = starts[owner_rows] + within
    global_live = within < counts[owner_rows]
    targets = row_id * WORK + jnp.arange(WORK, dtype=jnp.int32)
    matches = global_live[None, :] & (global_rank[None, :] == targets[:, None])
    source = jnp.sum(jnp.where(matches, global_ids[None, :], 0), axis=1)
    held = everyone[source]
    held_pairs = pair_index[source]
    held_live = jnp.ones((WORK,), dtype=bool)
    halfway = jnp.einsum(
        "scb,qdb->sqcd",
        lax.all_gather(held, "col", axis=1, tiled=True),
        full_factors,
        preferred_element_type=jnp.float32,
    ).astype(jnp.bfloat16)
    ladder = lax.psum_scatter(
        jnp.einsum("qac,sqcd->asd", full_factors, halfway, preferred_element_type=jnp.float32),
        "col",
        scatter_dimension=0,
        tiled=True,
    )
    ladder = jnp.transpose(ladder, (1, 0, 2))
    row_energy = lax.dynamic_slice_in_dim(vir_energy, col_id * col_rows, col_rows, 0)
    occupied = jnp.arange(occ_energy.shape[0], dtype=jnp.int32)
    picks = (held_pairs[:, :, None] == occupied[None, None, :]).astype(jnp.float32)
    pair_energy = jnp.sum(picks * occ_energy[None, None, :], axis=(1, 2))
    denominator = row_energy[None, :, None] + vir_energy[None, None, :] - pair_energy[:, None, None]
    amps_float = held.astype(jnp.float32)
    updated = amps_float - (ladder + denominator * amps_float) / (denominator + level_shift)
    updated = jnp.where(held_live[:, None, None], updated, 0.0).astype(jnp.bfloat16)
    returned = lax.all_gather(updated, "row", axis=0, tiled=True)
    chosen = jnp.clip(own_rank, 0, returned.shape[0] - 1)
    return jnp.where(own_live[:, None, None], returned[chosen], jnp.zeros((), jnp.bfloat16))


def solution(mesh):
    in_specs = (P("row", "col", None), P("col", "row", None), P(), P(), P(), P())
    out_specs = P("row", "col", None)
    return jax.shard_map(
        per_device, mesh=mesh, in_specs=in_specs, out_specs=out_specs, check_vma=False
    )
```

profile of v0, /device:TPU:0, one launch (start us, length us, event | category | flops | bytes accessed | tf_op | source)
XLA Modules:
  0.0 314.6 jit_solution(13453054312914106215)
XLA Ops:
  6.5 0.7 all-gather.6.cloned.1.call-update
  7.3 0.7 all-gather.8.cloned.1.call-update
  8.1 1.3 gather_fusion
  9.4 0.8 reduce-window.9
  10.2 0.7 bitcast_subtract_fusion
  10.9 0.7 gather_fusion.1
  11.8 37.6 %all-gather.6.cloned.1.call-done = bf16[16,96,768]{2,1,0:T(8,128)(2,1)} async-done(((bf16[4,96,768]{2,1,0:T(8,128)(2,1)}), bf16[16,96,768]{2,1,0:T(8,128)(2,1)}) %all-gather.6.cloned.1.call-update) | async-done | bytes 2359312 | tf_op jit(solution)/shard_map/all_gather | solution.py:22
  49.4 2.9 gather_fusion.2
  52.4 55.9 %all-gather.8.cloned.1.call-done = bf16[4,768,768]{2,1,0:T(8,128)(2,1)} async-done(((bf16[4,192,768]{2,1,0:T(8,128)(2,1)}), bf16[4,768,768]{2,1,0:T(8,128)(2,1)}) %all-gather.8.cloned.1.call-update) | async-done | bytes 4718608 | tf_op jit(solution)/shard_map/all_gather | solution.py:17
  108.3 33.3 %all-gather.12.cloned.1.call-done = bf16[2,768,768]{2,1,0:T(8,128)(2,1)} async-done(((bf16[2,96,768]{2,1,0:T(8,128)(2,1)}), bf16[2,768,768]{2,1,0:T(8,128)(2,1)}) %all-gather.12.cloned.1.call-update) | async-done | bytes 2359312 | tf_op jit(solution)/shard_map/all_gather | solution.py:37
  141.6 10.3 %fusion.4 = bf16[2,768,4,768]{3,1,2,0:T(8,128)(2,1)S(1)} fusion(bf16[4,768,768]{2,1,0:T(8,128)(2,1)} %all-gather.8.cloned.1.call-done, bf16[2,768,768]{2,1,0:T(8,128)(2,1)} %all-gather.12.cloned.1.call-done), kind=kOutput, calls=%fused_computation.9 | convolution fusion | flops 7247757312 | bytes 16515072 | tf_op jit(solution)/shard_map/scb,qdb->sqcd/dot_general | solution.py:35
  152.0 9.3 %fusion.7 = f32[768,2,768]{0,2,1:T(8,128)} fusion(bf16[4,768,768]{2,1,0:T(8,128)(2,1)S(1)} %copy-done.5, bf16[2,768,4,768]{3,1,2,0:T(8,128)(2,1)S(1)} %fusion.4), kind=kOutput, calls=%fused_computation.12 | convolution fusion | flops 7247757312 | bytes 18874368 | tf_op jit(solution)/shard_map/qac,sqcd->asd/dot_general | solution.py:42
  161.3 8.2 %copy.17 = f32[768,2,768]{2,1,0:T(2,128)} copy(f32[768,2,768]{0,2,1:T(8,128)} %fusion.7) | data formatting | bytes 9437184 | tf_op jit(solution)/shard_map/qac,sqcd->asd/dot_general | solution.py:42
  170.8 0.6 dynamic-slice
  172.3 102.9 %all-reduce.3.cloned.1.call-done = f32[768,2,768]{2,1,0:T(2,128)} async-done(((f32[768,2,768]{2,1,0:T(2,128)}), f32[768,2,768]{2,1,0:T(2,128)}) %all-reduce.3.cloned.1.call-update) | async-done | bytes 4718608
  275.2 1.1 constant_dynamic-slice_fusion
  276.4 1.0 fusion.12
  277.3 0.6 dynamic_slice.11
  277.9 0.6 dynamic_slice.9
  278.6 0.6 fusion.19
  279.1 0.6 iota_compare_fusion
  279.8 25.5 %all-gather.10.cloned.1.call-done = bf16[8,96,768]{2,1,0:T(8,128)(2,1)} async-done(((bf16[2,96,768]{2,1,0:T(8,128)(2,1)}), bf16[8,96,768]{2,1,0:T(8,128)(2,1)}) %all-gather.10.cloned.1.call-update) | async-done | bytes 1179664 | tf_op jit(solution)/shard_map/all_gather | solution.py:56
  305.3 1.9 gather_fusion.4
  307.1 0.9 broadcast_select_fusion
  (36 shorter events, 2.0 us)
Async XLA Ops:
  6.5 42.9 %all-gather.6.cloned.1.call-start = ((), (), s32[]{:S(2)}) async-start(), calls=%async_computation | async-start | bytes 2949120 | tf_op jit(solution)/shard_map/all_gather | solution.py:22
  7.3 101.1 %all-gather.8.cloned.1.call-start = ((), (), s32[]{:S(2)}) async-start(), calls=%async_computation.1 | async-start | bytes 5898240 | tf_op jit(solution)/shard_map/all_gather | solution.py:17
  8.0 133.6 %all-gather.12.cloned.1.call-start = ((), (), s32[]{:S(2)}) async-start(), calls=%async_computation.3 | async-start | bytes 2654208 | tf_op jit(solution)/shard_map/all_gather | solution.py:37
  52.4 222.9 %all-reduce.3.cloned.1.call-start = ((), (), s32[]{:S(2)}) async-start(), calls=%async_computation.4 | async-start | bytes 9437184
  141.6 10.3 %copy-start.5 = (bf16[4,768,768]{2,1,0:T(8,128)(2,1)S(1)}, bf16[4,768,768]{2,1,0:T(8,128)(2,1)}, u32[]{:S(2)}) copy-start(bf16[4,768,768]{2,1,0:T(8,128)(2,1)} %all-gather.8.cloned.1.call-done) | copy-start | bytes 14155780
  169.5 0.7 copy-start.3
  169.5 1.3 copy-start.6
  169.5 2.5 copy-start.2
  169.5 2.6 copy-start.4
  169.5 106.8 %copy-start.1 = (bf16[2,96,768]{2,1,0:T(8,128)(2,1)S(1)}, bf16[2,96,768]{2,1,0:T(8,128)(2,1)}, u32[]{:S(2)}) copy-start(bf16[2,96,768]{2,1,0:T(8,128)(2,1)} %gather_fusion.2) | copy-start | bytes 884740
  169.5 108.4 %copy-start = (s32[4]{0:T(128)S(1)}, s32[4]{0:T(128)}, u32[]{:S(2)}) copy-start(s32[4]{0:T(128)} %param.8) | copy-start | bytes 52
  169.6 135.7 %all-gather.10.cloned.1.call-start = ((), (), s32[]{:S(2)}) async-start(), calls=%async_computation.2 | async-start | bytes 1474560 | tf_op jit(solution)/shard_map/all_gather | solution.py:56
Sparse Core Ops, SparseCore 0:
  9.2 40.1 all-gather.5
  51.2 57.0 all-gather.7
  110.0 31.6 all-gather.11
  169.7 105.4 all-reduce.2
  277.5 27.7 all-gather.9
where the time goes:
time: 315 us
  waiting for transfers between devices  257 us (82%)
  matrix products  19.6 us (6%)
  local copies, waits for them, and re-layouts  19.2 us (6%)
  between operations  13.9 us (4%)
  other arithmetic  5.08 us (2%)
    unnamed x6, waiting for transfers between devices  104 us
    all_gather x1, waiting for transfers between devices, per_device(): full_factors = lax.all_gather(factors, 'row', axis=1, tiled=True)  55.9 us
    all_gather x1, waiting for transfers between devices, per_device(): everyone = lax.all_gather(amplitudes, 'row', axis=0, tiled=True)  37.6 us
    all_gather x1, waiting for transfers between devices, per_device(): lax.all_gather(held, 'col', axis=1, tiled=True)  33.3 us
    all_gather x1, waiting for transfers between devices, per_device(): returned = lax.all_gather(updated, 'row', axis=0, tiled=True)  25.5 us
    dot_general x1, matrix products, per_device(): jnp.einsum('scb,qdb->sqcd', lax.all_gather(held, 'col', axis=1, tiled=Tru...  10.3 us
    dot_general x1, matrix products, per_device(): jnp.einsum('qac,sqcd->asd', full_factors, halfway, preferred_element_type...  9.32 us
    dot_general x1, local copies, waits for them, and re-layouts, per_device(): jnp.einsum('qac,sqcd->asd', full_factors, halfway, preferred_element_type...  8.23 us
  transfers between devices with their start and end apart: 5, of which 5 were waited for; matrix products, arithmetic and copies ran while one was open for 3% of the time, Pallas kernels for 0%

commit v1 on v0

v1 whole, which is shorter than its diff:
```python
import functools

import jax
import jax.numpy as jnp
from jax import lax
from jax.experimental import pallas as pl
from jax.experimental.pallas import tpu as pltpu
from jax.sharding import PartitionSpec as P

WORK = 2
level_shift = 1.0
MESH = pl.DeviceIdType.MESH


def rank_range(pos, n, slots):
    total = WORK * n
    if isinstance(pos, int):
        return max(pos, total - slots * (n - pos)), min(slots * (pos + 1), total - (n - pos - 1))
    low = jnp.maximum(pos, total - slots * (n - pos))
    high = jnp.minimum(slots * (pos + 1), total - (n - pos - 1))
    return low, high


def reach_of(n, slots):
    reach = 0
    for pos in range(n):
        low, high = rank_range(pos, n, slots)
        reach = max([reach] + [abs(k // WORK - pos) for k in range(low, high)])
    return reach


def kernel(n, m, reach, amps, factors, counts, pairs, occ, vir, out,
           full, held, half, acc, stage, shuf, sib_out, sib_in, z_out, z_in, ret,
           l_send, l_recv, s_send, s_recv, t_send, t_recv, f_send, f_recv,
           b_send, b_recv, z_send, z_recv, r_send, r_recv):
    slots, rows, size = amps.shape
    vectors, block = factors.shape[0], factors.shape[1]
    nz = m // 2
    row, col = lax.axis_index("row"), lax.axis_index("col")
    z, core = col // 2, col % 2
    sibling = z * 2 + 1 - core
    pos = row // 2 + (row % 2) * (n - 1 - 2 * (row // 2))

    def row_at(p):
        if isinstance(p, int):
            return 2 * p if p < n // 2 else 2 * (n - 1 - p) + 1
        back = p // (n // 2)
        return (1 - back) * 2 * p + back * (2 * (n - 1 - p) + 1)

    def remote(src, dst, send, recv, **where):
        return pltpu.make_async_remote_copy(
            src_ref=src, dst_ref=dst, send_sem=send, recv_sem=recv, device_id=where, device_id_type=MESH)

    barrier = pltpu.get_barrier_semaphore()
    for step in range(1, n):
        pl.semaphore_signal(barrier, inc=1, device_id={"row": (row + step) % n}, device_id_type=MESH)
    for step in range(1, m):
        pl.semaphore_signal(barrier, inc=1, device_id={"col": (col + step) % m}, device_id_type=MESH)

    count_at = [counts[row_at(p)] for p in range(n)]
    start_at, running = [], jnp.int32(0)
    for p in range(n):
        start_at.append(running)
        running = running + count_at[p]

    def lookup(values, p):
        found = jnp.int32(0)
        for i in range(n):
            found = jnp.where(p == i, values[i], found)
        return found

    own_start, own_count = lookup(start_at, pos), lookup(count_at, pos)

    def owner_of(rank):
        src = jnp.int32(0)
        for p in range(n - 1):
            src = src + jnp.where(start_at[p] + count_at[p] <= rank, 1, 0)
        return src

    def feasible(p, worker, j):
        low, high = rank_range(p, n, slots)
        rank = worker * WORK + j
        return (p >= 0) & (p < n) & (worker >= 0) & (worker < n) & (rank >= low) & (rank < high)

    shifts = [d for d in range(-reach, reach + 1) if d != 0]
    for j in range(WORK):
        for d in shifts:
            slot = jnp.clip((pos + d) * WORK + j - own_start, 0, slots - 1)
            stage[d + reach, j] = amps[slot]
        shuf[reach, j] = amps[jnp.clip(pos * WORK + j - own_start, 0, slots - 1)]

    pl.semaphore_wait(barrier, n + m - 2)

    def shuffle(j, d):
        target = row_at((pos + d + n) % n)
        return remote(stage.at[d + reach, j], shuf.at[reach - d, j], s_send.at[d + reach, j], s_recv.at[reach - d, j],
                      row=target)

    def give_back(j, d):
        target = row_at((pos + d + n) % n)
        return remote(ret.at[reach, j], ret.at[reach - d, j], r_send.at[d + reach, j], r_recv.at[reach - d, j],
                      row=target)

    for j in range(WORK):
        for d in shifts:
            pl.when(feasible(pos, pos + d, j))(lambda j=j, d=d: shuffle(j, d).start())

    steps = n // 2
    part = block // 2

    def ring(step, q, way):
        move = 1 if way == 0 else -1
        origin = row_at((pos - move * step + n) % n)
        target = row_at((pos + move + n) % n)
        src = factors.at[q] if step == 0 else full.at[q, origin]
        dst = full.at[q, origin]
        if step == steps - 1:
            cut = pl.ds(way * part, part)
            src, dst = src.at[cut], dst.at[cut]
        return remote(src, dst, l_send.at[way, step, q], l_recv.at[way, step, q], row=target)

    def group(t):
        for step in range(steps - 1, -1, -1):
            q = t - 2 * step
            if 0 <= q < vectors:
                for way in range(2):
                    if step > 0:
                        ring(step - 1, q, way).wait_recv()
                    ring(step, q, way).start()

    groups = vectors + 2 * (steps - 1)
    ahead = 2 * (steps - 1)
    for t in range(min(2, groups)):
        group(t)

    def own_block(q, _):
        full[q, row] = factors[q]
        return 0

    lax.fori_loop(0, vectors, own_block, 0)

    def along(j, o):
        return remote(held.at[j, col], held.at[j, col], t_send.at[j, o], t_recv.at[j, o],
                      col=((z + o) % nz) * 2 + core)

    def across(j, o):
        from_z = (z - o + nz) % nz
        src = from_z * 2 + core
        return remote(held.at[j, src], held.at[j, src], f_send.at[j, o], f_recv.at[j, o], col=sibling)

    for j in range(WORK):
        for d in shifts:
            pl.when(feasible(pos - d, pos, j))(lambda j=j, d=d: shuffle(j, d).wait_recv())
        src = owner_of(pos * WORK + j) - pos
        chosen = shuf[reach, j]
        for d in shifts:
            chosen = jnp.where(src == d, shuf[d + reach, j], chosen)
        held[j, col] = chosen
        for o in range(1, nz):
            along(j, o).start()
        across(j, 0).start()

    for t in range(2, min(ahead + 1, groups)):
        group(t)
    for j in range(WORK):
        for o in range(1, nz):
            along(j, o).wait_recv()
            across(j, o).start()
    if ahead + 1 < groups:
        group(ahead + 1)

    tile = size // 2

    def pair_step(q, j):
        def first(i, _):
            at = pl.ds(pl.multiple_of(i * tile, tile), tile)
            lhs = held.at[j].reshape(size, size)[at, :]
            rhs = full[q].reshape(size, size)
            half[at, :] = lax.dot_general(
                lhs, rhs, (((1,), (1,)), ((), ())), preferred_element_type=jnp.float32).astype(jnp.bfloat16)
            return 0

        def second(i, _):
            at = pl.ds(pl.multiple_of(i * tile, tile), tile)
            lhs = full.at[q].reshape(size, size)[at, :]
            value = jnp.dot(lhs, half[...], preferred_element_type=jnp.float32)
            if q == 0:
                acc[j, at, :] = value
            else:
                acc[j, at, :] += value
            return 0

        lax.fori_loop(0, size // tile, first, 0)
        lax.fori_loop(0, size // tile, second, 0)

    def rows_of(c):
        return pl.ds(pl.multiple_of(c * rows, rows), rows)

    def to_sibling(j):
        return remote(sib_out.at[j], sib_in.at[j], b_send.at[j], b_recv.at[j], col=sibling)

    def to_owner(j, o):
        return remote(z_out.at[j, o], z_in.at[j, o], z_send.at[j, o], z_recv.at[j, o],
                      col=((z + o) % nz) * 2 + core)

    def share(j):
        for k in range(nz):
            sib_out[j, k] = acc[j, rows_of(2 * k + 1 - core), :].astype(jnp.bfloat16)
        to_sibling(j).start()

    def spread(j):
        to_sibling(j).wait_recv()
        for o in range(1, nz):
            k = (z + o) % nz
            total = acc[j, rows_of(2 * k + core), :] + sib_in[j, k].astype(jnp.float32)
            z_out[j, o] = total.astype(jnp.bfloat16)
            to_owner(j, o).start()

    def finish(j):
        rank = pos * WORK + j
        src = owner_of(rank)
        slot = rank - lookup(start_at, src)
        pair = jnp.clip(lookup([row_at(p) for p in range(n)], src) * slots + slot, 0, n * slots - 1)
        energy = occ[pairs[pair, 0]] + occ[pairs[pair, 1]]
        here = lax.broadcasted_iota(jnp.int32, (rows, size), 0) + col * rows
        there = lax.broadcasted_iota(jnp.int32, (rows, size), 1)
        levels = jnp.broadcast_to(vir[...], (rows, size))
        mine = jnp.sum(jnp.where(here == there, levels, 0.0), axis=1, keepdims=True)
        denominator = mine + levels - energy
        ladder = acc[j, rows_of(col), :] + sib_in[j, z].astype(jnp.float32)
        for o in range(1, nz):
            to_owner(j, o).wait_recv()
            ladder = ladder + z_in[j, o].astype(jnp.float32)
        t = held[j, col].astype(jnp.float32)
        new = t - (ladder + denominator * t) / (denominator + level_shift)
        ret[reach, j] = new.astype(jnp.bfloat16)
        for d in shifts:
            pl.when(feasible(pos + d, pos, j))(lambda j=j, d=d: give_back(j, d).start())

    for q in range(vectors):
        t = q + ahead + 1
        if q > 0 and t < groups:
            group(t)
        for way in range(2):
            ring(steps - 1, q, way).wait_recv()
        for j in range(WORK):
            if q == 0:
                for o in range(nz):
                    across(j, o).wait_recv()
            pair_step(q, j)
            if q == vectors - 1:
                share(j)
                if j > 0:
                    spread(j - 1)
    spread(WORK - 1)
    for j in range(WORK):
        finish(j)
    for j in range(WORK):
        for d in shifts:
            pl.when(feasible(pos, pos + d, j))(lambda j=j, d=d: give_back(j, -d).wait_recv())
    for s in range(slots):
        rank = own_start + s
        where = jnp.clip(rank // WORK - pos + reach, 0, 2 * reach)
        value = ret[where, jnp.clip(rank % WORK, 0, WORK - 1)]
        out[s] = jnp.where(s < own_count, value, jnp.zeros_like(value))

    for j in range(WORK):
        for d in shifts:
            pl.when(feasible(pos, pos + d, j))(lambda j=j, d=d: shuffle(j, d).wait_send())
            pl.when(feasible(pos + d, pos, j))(lambda j=j, d=d: give_back(j, d).wait_send())
        for o in range(1, nz):
            along(j, o).wait_send()
            to_owner(j, o).wait_send()
        for o in range(nz):
            across(j, o).wait_send()
        to_sibling(j).wait_send()
    for q in range(vectors):
        for step in range(steps):
            for way in range(2):
                ring(step, q, way).wait_send()


def solution(mesh):
    n, m = mesh.shape["row"], mesh.shape["col"]

    def per_device(amplitudes, factors, counts, pair_index, occ_energy, vir_energy):
        slots, rows, size = amplitudes.shape
        vectors, block, _ = factors.shape
        reach = reach_of(n, slots)
        span, nz, steps = 2 * reach + 1, m // 2, n // 2
        bf16, f32 = jnp.bfloat16, jnp.float32
        dma = pltpu.SemaphoreType.DMA
        vmem, smem = pl.BlockSpec(memory_space=pltpu.VMEM), pl.BlockSpec(memory_space=pltpu.SMEM)
        flops = 4 * vectors * WORK * size ** 3
        return pl.pallas_call(
            functools.partial(kernel, n, m, reach),
            out_shape=jax.ShapeDtypeStruct((slots, rows, size), bf16),
            in_specs=[vmem, vmem, smem, smem, smem, vmem],
            out_specs=vmem,
            scratch_shapes=[
                pltpu.VMEM((vectors, n, block, size), bf16),
                pltpu.VMEM((WORK, m, rows, size), bf16),
                pltpu.VMEM((size, size), bf16),
                pltpu.VMEM((WORK, size, size), f32),
                pltpu.VMEM((span, WORK, rows, size), bf16),
                pltpu.VMEM((span, WORK, rows, size), bf16),
                pltpu.VMEM((WORK, nz, rows, size), bf16),
                pltpu.VMEM((WORK, nz, rows, size), bf16),
                pltpu.VMEM((WORK, nz, rows, size), bf16),
                pltpu.VMEM((WORK, nz, rows, size), bf16),
                pltpu.VMEM((span, WORK, rows, size), bf16),
                dma((2, steps, vectors)), dma((2, steps, vectors)),
                dma((span, WORK)), dma((span, WORK)),
                dma((WORK, nz)), dma((WORK, nz)),
                dma((WORK, nz)), dma((WORK, nz)),
                dma((WORK,)), dma((WORK,)),
                dma((WORK, nz)), dma((WORK, nz)),
                dma((span, WORK)), dma((span, WORK)),
            ],
            cost_estimate=pl.CostEstimate(flops=flops, bytes_accessed=2 * vectors * size * size, transcendentals=0),
            compiler_params=pltpu.CompilerParams(
                collective_id=0, has_side_effects=True, vmem_limit_bytes=56 * 2 ** 20),
        )(amplitudes, factors, counts, pair_index, occ_energy, vir_energy.reshape(1, size))

    in_specs = (P("row", "col", None), P("col", "row", None), P(), P(), P(), P())
    return jax.shard_map(
        per_device, mesh=mesh, in_specs=in_specs, out_specs=P("row", "col", None), check_vma=False)
```

time: 315 us -> 98.5 us (0.31)
  waiting for transfers between devices: 257 us -> 0 us
  Pallas kernels: 0 us -> 92.8 us
  matrix products: 19.6 us -> 0 us
  local copies, waits for them, and re-layouts: 19.2 us -> 4.55 us
  between operations: 13.9 us -> 0.01 us
  other arithmetic: 5.08 us -> 0 us
    all_gather x4 -> x0, waiting for transfers between devices: 152 us -> none  [the longest x1 55.9 us: per_device(): full_factors = lax.all_gather(factors, 'row', axis=1, tiled=True)]
    unnamed x6 -> x0, waiting for transfers between devices: 104 us -> none
    pallas_call x0 -> x1, Pallas kernels: none -> 92.8 us  [per_device(): pl.pallas_call(functools.partial(kernel, n, m, reach), out_shape=jax.Shap...]
    dot_general x2 -> x0, matrix products: 19.6 us -> none  [the longest x1 10.3 us: per_device(): jnp.einsum('scb,qdb->sqcd', lax.all_gather(held, 'col', axis=1, tiled=Tru...]
    dot_general x1 -> x0, local copies, waits for them, and re-layouts: 8.23 us -> none  [per_device(): jnp.einsum('qac,sqcd->asd', full_factors, halfway, preferred_element_type...]
    gather x5 -> x0, local copies, waits for them, and re-layouts: 7.32 us -> none  [the longest x1 2.94 us: per_device(): held = everyone[source]]
  transfers between devices with their start and end apart: 5 -> 0, of which waited for: 5 -> 0; matrix products, arithmetic and copies ran while one was open for 3% -> 0% of each run, Pallas kernels for 0% -> 0%
where the time goes in v1:
time: 98.5 us; the launch traced here: 97.4 us
  Pallas kernels  92.8 us (94%)
  local copies, waits for them, and re-layouts  4.55 us (5%)
    pallas_call x1, Pallas kernels, per_device(): pl.pallas_call(functools.partial(kernel, n, m, reach), out_shape=jax.Shap...  92.8 us
    unnamed x2, local copies, waits for them, and re-layouts  3.27 us

profile of v1, /device:TPU:0, one launch (start us, length us, event | category | flops | bytes accessed | tf_op | source)
XLA Modules:
  0.0 97.4 jit_solution(14142010863097702456)
XLA Ops:
  0.0 1.3 %reshape.3.vir = f32[1,768]{1,0:T(1,128)} reshape(f32[768]{0:T(1024)} %param.11) | data formatting | bytes 6144 | tf_op jit(solution)/shard_map/reshape | solution.py:323
  1.3 1.4 %copy.7.pairs = s32[16,2]{1,0:T(8,128)} copy(s32[16,2]{0,1:T(2,128)} %param.9) | data formatting | bytes 256 | tf_op args[3]
  2.6 92.8 %shard_map.64 = bf16[4,96,768]{2,1,0:T(8,128)(2,1)} custom-call(bf16[4,96,768]{2,1,0:T(8,128)(2,1)} %amps.1, bf16[4,192,768]{2,1,0:T(8,128)(2,1)} %factors.1, s32[4]{0:T(128)} %counts.1, s32[16,2]{1,0:T(8,128)} %copy.7.pairs, f32[24]{0:T(128)} %occ.1, f32[1,768]{1,0:T(1,128)} %reshape.3.vir), custom_call_target="tpu_custom_call" | custom-call | flops 14495514624 | bytes 4718592 | tf_op jit(solution)/shard_map/pallas_call | solution.py:295
  95.5 1.9 %copy.9 = bf16[4,96,768]{2,1,0:T(8,128)(2,1)} copy(bf16[4,96,768]{2,1,0:T(8,128)(2,1)} %shard_map.64) | data formatting | bytes 1179648

commit v2 on v1

--- a/solution.py
+++ b/solution.py
@@ -139,14 +139,32 @@
 
     lax.fori_loop(0, vectors, own_block, 0)
 
-    def along(j, o):
-        return remote(held.at[j, col], held.at[j, col], t_send.at[j, o], t_recv.at[j, o],
-                      col=((z + o) % nz) * 2 + core)
-
-    def across(j, o):
-        from_z = (z - o + nz) % nz
-        src = from_z * 2 + core
-        return remote(held.at[j, src], held.at[j, src], f_send.at[j, o], f_recv.at[j, o], col=sibling)
+    def passed(h, way):
+        return z - h if way == 0 else z + h
+
+    def arrives(h, way):
+        return passed(h + 1, way) >= 0 if way == 0 else passed(h + 1, way) < nz
+
+    def leaves(h, way):
+        there = passed(h, way) >= 0 if way == 0 else passed(h, way) < nz
+        return there & (z + 1 < nz if way == 0 else z > 0)
+
+    def along(j, h, way):
+        src = passed(h, way) * 2 + core
+        target = (jnp.minimum(z + 1, nz - 1) if way == 0 else jnp.maximum(z - 1, 0)) * 2 + core
+        return remote(held.at[j, src], held.at[j, src], t_send.at[j, way, h], t_recv.at[j, way, h], col=target)
+
+    def across(j, h, way):
+        src = passed(h, way) * 2 + core
+        return remote(held.at[j, src], held.at[j, src], f_send.at[j, way, h], f_recv.at[j, way, h], col=sibling)
+
+    def hop(j, h, way):
+        @pl.when(arrives(h - 1, way))
+        def _():
+            along(j, h - 1, way).wait_recv()
+            if h < nz - 1:
+                pl.when(leaves(h, way))(lambda: along(j, h, way).start())
+            across(j, h, way).start()
 
     for j in range(WORK):
         for d in shifts:
@@ -156,22 +174,23 @@
         for d in shifts:
             chosen = jnp.where(src == d, shuf[d + reach, j], chosen)
         held[j, col] = chosen
-        for o in range(1, nz):
-            along(j, o).start()
-        across(j, 0).start()
-
-    for t in range(2, min(ahead + 1, groups)):
+        for way in range(2):
+            pl.when(leaves(0, way))(lambda j=j, way=way: along(j, 0, way).start())
+        across(j, 0, 0).start()
+
+    later = list(range(2, min(ahead + 2, groups)))
+    for h in range(1, nz):
+        for j in range(WORK):
+            for way in range(2):
+                hop(j, h, way)
+        if later:
+            group(later.pop(0))
+    for t in later:
         group(t)
-    for j in range(WORK):
-        for o in range(1, nz):
-            along(j, o).wait_recv()
-            across(j, o).start()
-    if ahead + 1 < groups:
-        group(ahead + 1)
 
     tile = size // 2
 
-    def pair_step(q, j):
+    def pair_first(q, j):
         def first(i, _):
             at = pl.ds(pl.multiple_of(i * tile, tile), tile)
             lhs = held.at[j].reshape(size, size)[at, :]
@@ -180,6 +199,9 @@
                 lhs, rhs, (((1,), (1,)), ((), ())), preferred_element_type=jnp.float32).astype(jnp.bfloat16)
             return 0
 
+        lax.fori_loop(0, size // tile, first, 0)
+
+    def pair_second(q, j):
         def second(i, _):
             at = pl.ds(pl.multiple_of(i * tile, tile), tile)
             lhs = full.at[q].reshape(size, size)[at, :]
@@ -190,7 +212,6 @@
                 acc[j, at, :] += value
             return 0
 
-        lax.fori_loop(0, size // tile, first, 0)
         lax.fori_loop(0, size // tile, second, 0)
 
     def rows_of(c):
@@ -199,38 +220,72 @@
     def to_sibling(j):
         return remote(sib_out.at[j], sib_in.at[j], b_send.at[j], b_recv.at[j], col=sibling)
 
-    def to_owner(j, o):
-        return remote(z_out.at[j, o], z_in.at[j, o], z_send.at[j, o], z_recv.at[j, o],
-                      col=((z + o) % nz) * 2 + core)
+    def onward(j, k, way):
+        target = (jnp.minimum(z + 1, nz - 1) if way == 0 else jnp.maximum(z - 1, 0)) * 2 + core
+        slot = k if way == 0 else jnp.where(k == z - 1, nz, k)
+        return remote(z_out.at[j, k], z_in.at[j, slot], z_send.at[j, k], z_recv.at[j, slot], col=target)
+
+    def incoming(j, slot):
+        sent = min(slot, nz - 1) if isinstance(slot, int) else slot
+        return remote(z_out.at[j, sent], z_in.at[j, slot], z_send.at[j, sent], z_recv.at[j, slot], col=sibling)
 
     def share(j):
         for k in range(nz):
             sib_out[j, k] = acc[j, rows_of(2 * k + 1 - core), :].astype(jnp.bfloat16)
         to_sibling(j).start()
 
+    def chain(j, action):
+        for i in range(nz - 1):
+            for way in range(2):
+                k = nz - 1 - i if way == 0 else i
+                ahead_of = (k > z) if way == 0 else (k < z)
+                first = (z == 0) if way == 0 else (z == nz - 1)
+                action(j, k, way, ahead_of, first)
+
+    def begin(j, k, way, ahead_of, first):
+        @pl.when(ahead_of & first)
+        def _():
+            total = acc[j, rows_of(2 * k + core), :] + sib_in[j, k].astype(jnp.float32)
+            z_out[j, k] = total.astype(jnp.bfloat16)
+            onward(j, k, way).start()
+
+    def go_on(j, k, way, ahead_of, first):
+        @pl.when(ahead_of & jnp.logical_not(first))
+        def _():
+            total = acc[j, rows_of(2 * k + core), :] + sib_in[j, k].astype(jnp.float32)
+            incoming(j, k).wait_recv()
+            z_out[j, k] = (total + z_in[j, k].astype(jnp.float32)).astype(jnp.bfloat16)
+            onward(j, k, way).start()
+
     def spread(j):
         to_sibling(j).wait_recv()
-        for o in range(1, nz):
-            k = (z + o) % nz
-            total = acc[j, rows_of(2 * k + core), :] + sib_in[j, k].astype(jnp.float32)
-            z_out[j, o] = total.astype(jnp.bfloat16)
-            to_owner(j, o).start()
+        chain(j, begin)
 
     def finish(j):
         rank = pos * WORK + j
         src = owner_of(rank)
         slot = rank - lookup(start_at, src)
         pair = jnp.clip(lookup([row_at(p) for p in range(n)], src) * slots + slot, 0, n * slots - 1)
-        energy = occ[pairs[pair, 0]] + occ[pairs[pair, 1]]
+        energy = occ[pairs[0, pair]] + occ[pairs[1, pair]]
         here = lax.broadcasted_iota(jnp.int32, (rows, size), 0) + col * rows
         there = lax.broadcasted_iota(jnp.int32, (rows, size), 1)
         levels = jnp.broadcast_to(vir[...], (rows, size))
         mine = jnp.sum(jnp.where(here == there, levels, 0.0), axis=1, keepdims=True)
         denominator = mine + levels - energy
-        ladder = acc[j, rows_of(col), :] + sib_in[j, z].astype(jnp.float32)
-        for o in range(1, nz):
-            to_owner(j, o).wait_recv()
-            ladder = ladder + z_in[j, o].astype(jnp.float32)
+        own = rows_of(col)
+        acc[j, own, :] += sib_in[j, z].astype(jnp.float32)
+
+        @pl.when(z > 0)
+        def _():
+            incoming(j, z).wait_recv()
+            acc[j, own, :] += z_in[j, z].astype(jnp.float32)
+
+        @pl.when(z < nz - 1)
+        def _():
+            incoming(j, nz).wait_recv()
+            acc[j, own, :] += z_in[j, nz].astype(jnp.float32)
+
+        ladder = acc[j, own, :]
         t = held[j, col].astype(jnp.float32)
         new = t - (ladder + denominator * t) / (denominator + level_shift)
         ret[reach, j] = new.astype(jnp.bfloat16)
@@ -245,16 +300,23 @@
             ring(steps - 1, q, way).wait_recv()
         for j in range(WORK):
             if q == 0:
-                for o in range(nz):
-                    across(j, o).wait_recv()
-            pair_step(q, j)
+                across(j, 0, 0).wait_recv()
+                for h in range(1, nz):
+                    for way in range(2):
+                        pl.when(arrives(h - 1, way))(lambda j=j, h=h, way=way: across(j, h, way).wait_recv())
+            pair_first(q, j)
+            if q == vectors - 1 and j > 0:
+                spread(j - 1)
+            pair_second(q, j)
             if q == vectors - 1:
                 share(j)
-                if j > 0:
-                    spread(j - 1)
+    for j in range(WORK - 1):
+        chain(j, go_on)
     spread(WORK - 1)
-    for j in range(WORK):
+    for j in range(WORK - 1):
         finish(j)
+    chain(WORK - 1, go_on)
+    finish(WORK - 1)
     for j in range(WORK):
         for d in shifts:
             pl.when(feasible(pos, pos + d, j))(lambda j=j, d=d: give_back(j, -d).wait_recv())
@@ -268,11 +330,13 @@
         for d in shifts:
             pl.when(feasible(pos, pos + d, j))(lambda j=j, d=d: shuffle(j, d).wait_send())
             pl.when(feasible(pos + d, pos, j))(lambda j=j, d=d: give_back(j, d).wait_send())
-        for o in range(1, nz):
-            along(j, o).wait_send()
-            to_owner(j, o).wait_send()
-        for o in range(nz):
-            across(j, o).wait_send()
+        across(j, 0, 0).wait_send()
+        for way in range(2):
+            for h in range(nz - 1):
+                pl.when(leaves(h, way))(lambda j=j, h=h, way=way: along(j, h, way).wait_send())
+                pl.when(arrives(h, way))(lambda j=j, h=h, way=way: across(j, h + 1, way).wait_send())
+        for k in range(nz):
+            pl.when(z != k)(lambda j=j, k=k: incoming(j, k).wait_send())
         to_sibling(j).wait_send()
     for q in range(vectors):
         for step in range(steps):
@@ -307,20 +371,20 @@
                 pltpu.VMEM((WORK, nz, rows, size), bf16),
                 pltpu.VMEM((WORK, nz, rows, size), bf16),
                 pltpu.VMEM((WORK, nz, rows, size), bf16),
-                pltpu.VMEM((WORK, nz, rows, size), bf16),
+                pltpu.VMEM((WORK, nz + 1, rows, size), bf16),
                 pltpu.VMEM((span, WORK, rows, size), bf16),
                 dma((2, steps, vectors)), dma((2, steps, vectors)),
                 dma((span, WORK)), dma((span, WORK)),
-                dma((WORK, nz)), dma((WORK, nz)),
-                dma((WORK, nz)), dma((WORK, nz)),
+                dma((WORK, 2, nz)), dma((WORK, 2, nz)),
+                dma((WORK, 2, nz)), dma((WORK, 2, nz)),
                 dma((WORK,)), dma((WORK,)),
-                dma((WORK, nz)), dma((WORK, nz)),
+                dma((WORK, nz)), dma((WORK, nz + 1)),
                 dma((span, WORK)), dma((span, WORK)),
             ],
             cost_estimate=pl.CostEstimate(flops=flops, bytes_accessed=2 * vectors * size * size, transcendentals=0),
             compiler_params=pltpu.CompilerParams(
                 collective_id=0, has_side_effects=True, vmem_limit_bytes=56 * 2 ** 20),
-        )(amplitudes, factors, counts, pair_index, occ_energy, vir_energy.reshape(1, size))
+        )(amplitudes, factors, counts, pair_index.T, occ_energy, vir_energy)
 
     in_specs = (P("row", "col", None), P("col", "row", None), P(), P(), P(), P())
     return jax.shard_map(

time: 98.5 us -> 103 us (1.046)
  Pallas kernels: 92.8 us -> 100 us
  local copies, waits for them, and re-layouts: 4.55 us -> 1.92 us
    pallas_call x1, Pallas kernels: 92.8 us -> 100 us  [per_device(): pl.pallas_call(functools.partial(kernel, n, m, reach), out_shape=jax.Shap...]
    unnamed x2 -> x1, local copies, waits for them, and re-layouts: 3.27 us -> 1.92 us
    reshape x1 -> x0, local copies, waits for them, and re-layouts: 1.28 us -> none  [per_device(): vir_energy.reshape(1, size)]
where the time goes in v2:
time: 103 us; the launch traced here: 102 us
  Pallas kernels  100 us (97%)
  local copies, waits for them, and re-layouts  1.92 us (2%)
    pallas_call x1, Pallas kernels, per_device(): pl.pallas_call(functools.partial(kernel, n, m, reach), out_shape=jax.Shap...  100 us

profile of v2, /device:TPU:0, one launch (start us, length us, event | category | flops | bytes accessed | tf_op | source)
XLA Modules:
  0.0 102.4 jit_solution(8644738398919879210)
XLA Ops:
  0.0 100.5 %shard_map.64 = bf16[4,96,768]{2,1,0:T(8,128)(2,1)} custom-call(bf16[4,96,768]{2,1,0:T(8,128)(2,1)} %amps.1, bf16[4,192,768]{2,1,0:T(8,128)(2,1)} %factors.1, s32[4]{0:T(128)} %counts.1, s32[2,16]{1,0:T(2,128)} %bitcast.1, f32[24]{0:T(128)} %occ.1, f32[768]{0:T(1024)} %vir.1), custom_call_target="tpu_custom_call" | custom-call | flops 14495514624 | bytes 4718592 | tf_op jit(solution)/shard_map/pallas_call | solution.py:359
  100.5 1.9 %copy.8 = bf16[4,96,768]{2,1,0:T(8,128)(2,1)} copy(bf16[4,96,768]{2,1,0:T(8,128)(2,1)} %shard_map.64) | data formatting | bytes 1179648

commit v3 on v2

--- a/solution.py
+++ b/solution.py
@@ -107,6 +107,7 @@
 
     steps = n // 2
     part = block // 2
+    lead = 3
 
     def ring(step, q, way):
         move = 1 if way == 0 else -1
@@ -121,16 +122,16 @@
 
     def group(t):
         for step in range(steps - 1, -1, -1):
-            q = t - 2 * step
+            q = t - lead * step
             if 0 <= q < vectors:
                 for way in range(2):
                     if step > 0:
                         ring(step - 1, q, way).wait_recv()
                     ring(step, q, way).start()
 
-    groups = vectors + 2 * (steps - 1)
-    ahead = 2 * (steps - 1)
-    for t in range(min(2, groups)):
+    groups = vectors + lead * (steps - 1)
+    ahead = lead * (steps - 1)
+    for t in range(min(lead, groups)):
         group(t)
 
     def own_block(q, _):
@@ -178,12 +179,12 @@
             pl.when(leaves(0, way))(lambda j=j, way=way: along(j, 0, way).start())
         across(j, 0, 0).start()
 
-    later = list(range(2, min(ahead + 2, groups)))
+    later = list(range(lead, min(ahead + 2, groups)))
     for h in range(1, nz):
         for j in range(WORK):
             for way in range(2):
                 hop(j, h, way)
-        if later:
+        if later and h > 1:
             group(later.pop(0))
     for t in later:
         group(t)
@@ -235,12 +236,17 @@
         to_sibling(j).start()
 
     def chain(j, action):
-        for i in range(nz - 1):
-            for way in range(2):
+        def one_way(way):
+            for i in range(nz - 1):
                 k = nz - 1 - i if way == 0 else i
                 ahead_of = (k > z) if way == 0 else (k < z)
                 first = (z == 0) if way == 0 else (z == nz - 1)
                 action(j, k, way, ahead_of, first)
+
+        low = z < nz // 2
+        pl.when(low)(lambda: one_way(0))
+        one_way(1)
+        pl.when(jnp.logical_not(low))(lambda: one_way(0))
 
     def begin(j, k, way, ahead_of, first):
         @pl.when(ahead_of & first)

time: 103 us -> 95.4 us (0.926)
  Pallas kernels: 100 us -> 93.3 us
    pallas_call x1, Pallas kernels: 100 us -> 93.3 us  [per_device(): pl.pallas_call(functools.partial(kernel, n, m, reach), out_shape=jax.Shap...]
where the time goes in v3:
time: 95.4 us; the launch traced here: 95.2 us
  Pallas kernels  93.3 us (98%)
  local copies, waits for them, and re-layouts  1.92 us (2%)
    pallas_call x1, Pallas kernels, per_device(): pl.pallas_call(functools.partial(kernel, n, m, reach), out_shape=jax.Shap...  93.3 us
    unnamed x1, local copies, waits for them, and re-layouts  1.92 us

profile of v3, /device:TPU:0, one launch (start us, length us, event | category | flops | bytes accessed | tf_op | source)
XLA Modules:
  0.0 95.2 jit_solution(1551935670880924477)
XLA Ops:
  0.0 93.3 %shard_map.64 = bf16[4,96,768]{2,1,0:T(8,128)(2,1)} custom-call(bf16[4,96,768]{2,1,0:T(8,128)(2,1)} %amps.1, bf16[4,192,768]{2,1,0:T(8,128)(2,1)} %factors.1, s32[4]{0:T(128)} %counts.1, s32[2,16]{1,0:T(2,128)} %bitcast.1, f32[24]{0:T(128)} %occ.1, f32[768]{0:T(1024)} %vir.1), custom_call_target="tpu_custom_call" | custom-call | flops 14495514624 | bytes 4718592 | tf_op jit(solution)/shard_map/pallas_call | solution.py:365
  93.3 1.9 %copy.8 = bf16[4,96,768]{2,1,0:T(8,128)(2,1)} copy(bf16[4,96,768]{2,1,0:T(8,128)(2,1)} %shard_map.64) | data formatting | bytes 1179648

commit v4 on v3

--- a/solution.py
+++ b/solution.py
@@ -189,31 +189,31 @@
     for t in later:
         group(t)
 
-    tile = size // 2
-
-    def pair_first(q, j):
+    tile = 256 if size % 256 == 0 else size
+
+    def both_first(q):
         def first(i, _):
             at = pl.ds(pl.multiple_of(i * tile, tile), tile)
-            lhs = held.at[j].reshape(size, size)[at, :]
-            rhs = full[q].reshape(size, size)
-            half[at, :] = lax.dot_general(
+            lhs = held[...].reshape(WORK * size, size)
+            rhs = full.at[q].reshape(size, size)[at, :]
+            half[:, at] = lax.dot_general(
                 lhs, rhs, (((1,), (1,)), ((), ())), preferred_element_type=jnp.float32).astype(jnp.bfloat16)
             return 0
 
         lax.fori_loop(0, size // tile, first, 0)
 
-    def pair_second(q, j):
+    def pair_second(q, j, low, high):
         def second(i, _):
             at = pl.ds(pl.multiple_of(i * tile, tile), tile)
-            lhs = full.at[q].reshape(size, size)[at, :]
-            value = jnp.dot(lhs, half[...], preferred_element_type=jnp.float32)
+            lhs = full[q].reshape(size, size)
+            value = jnp.dot(lhs, half[pl.ds(j * size, size), at], preferred_element_type=jnp.float32)
             if q == 0:
-                acc[j, at, :] = value
+                acc[j, :, at] = value
             else:
-                acc[j, at, :] += value
+                acc[j, :, at] += value
             return 0
 
-        lax.fori_loop(0, size // tile, second, 0)
+        lax.fori_loop(low, high, second, 0)
 
     def rows_of(c):
         return pl.ds(pl.multiple_of(c * rows, rows), rows)
@@ -304,16 +304,21 @@
             group(t)
         for way in range(2):
             ring(steps - 1, q, way).wait_recv()
-        for j in range(WORK):
-            if q == 0:
+        if q == 0:
+            for j in range(WORK):
                 across(j, 0, 0).wait_recv()
                 for h in range(1, nz):
                     for way in range(2):
                         pl.when(arrives(h - 1, way))(lambda j=j, h=h, way=way: across(j, h, way).wait_recv())
-            pair_first(q, j)
+        both_first(q)
+        for j in range(WORK):
+            tiles = size // tile
             if q == vectors - 1 and j > 0:
+                pair_second(q, j, 0, tiles // 2)
                 spread(j - 1)
-            pair_second(q, j)
+                pair_second(q, j, tiles // 2, tiles)
+            else:
+                pair_second(q, j, 0, tiles)
             if q == vectors - 1:
                 share(j)
     for j in range(WORK - 1):
@@ -370,7 +375,7 @@
             scratch_shapes=[
                 pltpu.VMEM((vectors, n, block, size), bf16),
                 pltpu.VMEM((WORK, m, rows, size), bf16),
-                pltpu.VMEM((size, size), bf16),
+                pltpu.VMEM((WORK * size, size), bf16),
                 pltpu.VMEM((WORK, size, size), f32),
                 pltpu.VMEM((span, WORK, rows, size), bf16),
                 pltpu.VMEM((span, WORK, rows, size), bf16),

time: 95.4 us -> 96.8 us (1.015)
  Pallas kernels: 93.3 us -> 94.7 us
    pallas_call x1, Pallas kernels: 93.3 us -> 94.7 us  [per_device(): pl.pallas_call(functools.partial(kernel, n, m, reach), out_shape=jax.Shap...]
where the time goes in v4:
time: 96.8 us; the launch traced here: 96.7 us
  Pallas kernels  94.7 us (98%)
  local copies, waits for them, and re-layouts  1.92 us (2%)
    pallas_call x1, Pallas kernels, per_device(): pl.pallas_call(functools.partial(kernel, n, m, reach), out_shape=jax.Shap...  94.7 us

profile of v4, /device:TPU:0, one launch (start us, length us, event | category | flops | bytes accessed | tf_op | source)
XLA Modules:
  0.0 96.7 jit_solution(18008137291445244371)
XLA Ops:
  0.0 94.7 %shard_map.64 = bf16[4,96,768]{2,1,0:T(8,128)(2,1)} custom-call(bf16[4,96,768]{2,1,0:T(8,128)(2,1)} %amps.1, bf16[4,192,768]{2,1,0:T(8,128)(2,1)} %factors.1, s32[4]{0:T(128)} %counts.1, s32[2,16]{1,0:T(2,128)} %bitcast.1, f32[24]{0:T(128)} %occ.1, f32[768]{0:T(1024)} %vir.1), custom_call_target="tpu_custom_call" | custom-call | flops 14495514624 | bytes 4718592 | tf_op jit(solution)/shard_map/pallas_call | solution.py:370
  94.8 1.9 %copy.8 = bf16[4,96,768]{2,1,0:T(8,128)(2,1)} copy(bf16[4,96,768]{2,1,0:T(8,128)(2,1)} %shard_map.64) | data formatting | bytes 1179648

commit v5 on v3

--- a/solution.py
+++ b/solution.py
@@ -30,9 +30,12 @@
 
 
 def kernel(n, m, reach, amps, factors, counts, pairs, occ, vir, out,
-           full, held, half, acc, stage, shuf, sib_out, sib_in, z_out, z_in, ret,
+           full, held, half, half_far, acc_s, acc_b, stage, shuf, sib_out_s, sib_out_b, sib_in_s, sib_in_b,
+           z_out_s, z_out_b, z_in_s, z_in_b, lad, ret,
            l_send, l_recv, s_send, s_recv, t_send, t_recv, f_send, f_recv,
            b_send, b_recv, z_send, z_recv, r_send, r_recv):
+    acc, sib_out, sib_in = (acc_s, acc_b), (sib_out_s, sib_out_b), (sib_in_s, sib_in_b)
+    z_out, z_in = (z_out_s, z_out_b), (z_in_s, z_in_b)
     slots, rows, size = amps.shape
     vectors, block = factors.shape[0], factors.shape[1]
     nz = m // 2
@@ -107,14 +110,15 @@
 
     steps = n // 2
     part = block // 2
-    lead = 3
+    lead = vectors
+
+    def place(step, way):
+        return 0 if step == 0 else (n - 1 if step == steps else 2 * step - 1 + way)
 
     def ring(step, q, way):
-        move = 1 if way == 0 else -1
-        origin = row_at((pos - move * step + n) % n)
-        target = row_at((pos + move + n) % n)
-        src = factors.at[q] if step == 0 else full.at[q, origin]
-        dst = full.at[q, origin]
+        target = row_at((pos + (1 if way == 0 else -1) + n) % n)
+        src = factors.at[q] if step == 0 else full.at[q, place(step, way)]
+        dst = full.at[q, place(step + 1, way)]
         if step == steps - 1:
             cut = pl.ds(way * part, part)
             src, dst = src.at[cut], dst.at[cut]
@@ -129,13 +133,11 @@
                         ring(step - 1, q, way).wait_recv()
                     ring(step, q, way).start()
 
-    groups = vectors + lead * (steps - 1)
-    ahead = lead * (steps - 1)
-    for t in range(min(lead, groups)):
+    for t in range(lead * (steps - 1)):
         group(t)
 
     def own_block(q, _):
-        full[q, row] = factors[q]
+        full[q, 0] = factors[q]
         return 0
 
     lax.fori_loop(0, vectors, own_block, 0)
@@ -179,93 +181,111 @@
             pl.when(leaves(0, way))(lambda j=j, way=way: along(j, 0, way).start())
         across(j, 0, 0).start()
 
-    later = list(range(lead, min(ahead + 2, groups)))
     for h in range(1, nz):
         for j in range(WORK):
             for way in range(2):
                 hop(j, h, way)
-        if later and h > 1:
-            group(later.pop(0))
-    for t in later:
-        group(t)
-
-    tile = size // 2
-
-    def pair_first(q, j):
-        def first(i, _):
-            at = pl.ds(pl.multiple_of(i * tile, tile), tile)
-            lhs = held.at[j].reshape(size, size)[at, :]
-            rhs = full[q].reshape(size, size)
-            half[at, :] = lax.dot_general(
-                lhs, rhs, (((1,), (1,)), ((), ())), preferred_element_type=jnp.float32).astype(jnp.bfloat16)
+
+    near = (n - 1) * block
+
+    def dot_t(x, y):
+        return lax.dot_general(x, y, (((1,), (1,)), ((), ())), preferred_element_type=jnp.float32)
+
+    def near_first(q):
+        def one(j, _):
+            value = dot_t(held[j].reshape(size, size), full[q, 0:n - 1].reshape(near, size))
+            half[q, j] = value.astype(jnp.bfloat16)
             return 0
 
-        lax.fori_loop(0, size // tile, first, 0)
-
-    def pair_second(q, j):
-        def second(i, _):
-            at = pl.ds(pl.multiple_of(i * tile, tile), tile)
-            lhs = full.at[q].reshape(size, size)[at, :]
-            value = jnp.dot(lhs, half[...], preferred_element_type=jnp.float32)
-            if q == 0:
-                acc[j, at, :] = value
-            else:
-                acc[j, at, :] += value
-            return 0
-
-        lax.fori_loop(0, size // tile, second, 0)
+        lax.fori_loop(0, WORK, one, 0)
+
+    def near_second(q, j):
+        value = jnp.dot(full[q, 0:n - 1].reshape(near, size), half[q, j], preferred_element_type=jnp.float32)
+        if q == 0:
+            acc_s[j, 0:near, :] = value
+        else:
+            acc_s[j, 0:near, :] += value
+
+    def far(q, j):
+        value = dot_t(held[j].reshape(size, size), full[q, n - 1])
+        half_far[...] = value.astype(jnp.bfloat16)
+        value = jnp.dot(full[q].reshape(size, size), half_far[...], preferred_element_type=jnp.float32)
+        corner = jnp.dot(full[q, n - 1], half[q, j], preferred_element_type=jnp.float32)
+        if q == 0:
+            acc_b[j] = value
+            acc_s[j, near:size, :] = corner
+        else:
+            acc_b[j] += value
+            acc_s[j, near:size, :] += corner
+
+    def place_of(b):
+        p = b // 2 + (b % 2) * (n - 1 - 2 * (b // 2))
+        d = (p - pos + n) % n
+        return jnp.where(d == n // 2, n - 1, jnp.where(d < n // 2, 2 * d, 2 * (n - d) - 1))
+
+    def is_far(c):
+        return place_of((c * rows) // block) == n - 1
 
     def rows_of(c):
-        return pl.ds(pl.multiple_of(c * rows, rows), rows)
-
-    def to_sibling(j):
-        return remote(sib_out.at[j], sib_in.at[j], b_send.at[j], b_recv.at[j], col=sibling)
-
-    def onward(j, k, way):
+        start = place_of((c * rows) // block) * block + (c * rows) % block
+        return pl.ds(pl.multiple_of(start, rows), rows)
+
+    def ready(stage_of, c):
+        if stage_of == 2:
+            return c >= 0
+        return is_far(c) if stage_of == 1 else jnp.logical_not(is_far(c))
+
+    def to_sibling(w, j, k):
+        return remote(sib_out[w].at[j, k], sib_in[w].at[j, k], b_send.at[w, j, k], b_recv.at[w, j, k], col=sibling)
+
+    def onward(w, j, k, way):
         target = (jnp.minimum(z + 1, nz - 1) if way == 0 else jnp.maximum(z - 1, 0)) * 2 + core
         slot = k if way == 0 else jnp.where(k == z - 1, nz, k)
-        return remote(z_out.at[j, k], z_in.at[j, slot], z_send.at[j, k], z_recv.at[j, slot], col=target)
-
-    def incoming(j, slot):
+        return remote(z_out[w].at[j, k], z_in[w].at[j, slot], z_send.at[w, j, k], z_recv.at[w, j, slot], col=target)
+
+    def incoming(w, j, slot):
         sent = min(slot, nz - 1) if isinstance(slot, int) else slot
-        return remote(z_out.at[j, sent], z_in.at[j, slot], z_send.at[j, sent], z_recv.at[j, slot], col=sibling)
-
-    def share(j):
+        return remote(z_out[w].at[j, sent], z_in[w].at[j, slot], z_send.at[w, j, sent], z_recv.at[w, j, slot],
+                      col=sibling)
+
+    def share(stage_of, j):
+        w = stage_of // 2
         for k in range(nz):
-            sib_out[j, k] = acc[j, rows_of(2 * k + 1 - core), :].astype(jnp.bfloat16)
-        to_sibling(j).start()
-
-    def chain(j, action):
+            c = 2 * k + 1 - core
+
+            @pl.when(ready(stage_of, c))
+            def _():
+                sib_out[w][j, k] = acc[w][j, rows_of(c), :].astype(jnp.bfloat16)
+                to_sibling(w, j, k).start()
+
+    def chain(stage_of, j, begins):
+        w = stage_of // 2
+
         def one_way(way):
             for i in range(nz - 1):
                 k = nz - 1 - i if way == 0 else i
-                ahead_of = (k > z) if way == 0 else (k < z)
+                c = 2 * k + core
                 first = (z == 0) if way == 0 else (z == nz - 1)
-                action(j, k, way, ahead_of, first)
-
-        low = z < nz // 2
-        pl.when(low)(lambda: one_way(0))
-        one_way(1)
-        pl.when(jnp.logical_not(low))(lambda: one_way(0))
-
-    def begin(j, k, way, ahead_of, first):
-        @pl.when(ahead_of & first)
-        def _():
-            total = acc[j, rows_of(2 * k + core), :] + sib_in[j, k].astype(jnp.float32)
-            z_out[j, k] = total.astype(jnp.bfloat16)
-            onward(j, k, way).start()
-
-    def go_on(j, k, way, ahead_of, first):
-        @pl.when(ahead_of & jnp.logical_not(first))
-        def _():
-            total = acc[j, rows_of(2 * k + core), :] + sib_in[j, k].astype(jnp.float32)
-            incoming(j, k).wait_recv()
-            z_out[j, k] = (total + z_in[j, k].astype(jnp.float32)).astype(jnp.bfloat16)
-            onward(j, k, way).start()
-
-    def spread(j):
-        to_sibling(j).wait_recv()
-        chain(j, begin)
+                first = first if begins else jnp.logical_not(first)
+
+                @pl.when(((k > z) if way == 0 else (k < z)) & first & ready(stage_of, c))
+                def _():
+                    to_sibling(w, j, k).wait_recv()
+                    total = acc[w][j, rows_of(c), :] + sib_in[w][j, k].astype(jnp.float32)
+                    if not begins:
+                        incoming(w, j, k).wait_recv()
+                        total = total + z_in[w][j, k].astype(jnp.float32)
+                    z_out[w][j, k] = total.astype(jnp.bfloat16)
+                    onward(w, j, k, way).start()
+
+        if begins:
+            one_way(0)
+            one_way(1)
+        else:
+            low = z < nz // 2
+            pl.when(low)(lambda: one_way(0))
+            one_way(1)
+            pl.when(jnp.logical_not(low))(lambda: one_way(0))
 
     def finish(j):
         rank = pos * WORK + j
@@ -279,50 +299,76 @@
         mine = jnp.sum(jnp.where(here == there, levels, 0.0), axis=1, keepdims=True)
         denominator = mine + levels - energy
         own = rows_of(col)
-        acc[j, own, :] += sib_in[j, z].astype(jnp.float32)
+        for w in range(2):
+            to_sibling(w, j, z).wait_recv()
+            acc[w][j, own, :] += sib_in[w][j, z].astype(jnp.float32)
 
         @pl.when(z > 0)
         def _():
-            incoming(j, z).wait_recv()
-            acc[j, own, :] += z_in[j, z].astype(jnp.float32)
+            for w in range(2):
+                incoming(w, j, z).wait_recv()
+                acc[w][j, own, :] += z_in[w][j, z].astype(jnp.float32)
 
         @pl.when(z < nz - 1)
         def _():
-            incoming(j, nz).wait_recv()
-            acc[j, own, :] += z_in[j, nz].astype(jnp.float32)
-
-        ladder = acc[j, own, :]
+            for w in range(2):
+                incoming(w, j, nz).wait_recv()
+                acc[w][j, own, :] += z_in[w][j, nz].astype(jnp.float32)
+
+        for b in range(n):
+            for i in range(n):
+                @pl.when(place_of(b) == i)
+                def _(b=b, i=i):
+                    if i < n - 1:
+                        piece = acc_s[j, own, i * block:(i + 1) * block]
+                    else:
+                        piece = acc_b[j, own, :]
+                    lad[:, b * block:(b + 1) * block] = piece
+        ladder = lad[...]
         t = held[j, col].astype(jnp.float32)
         new = t - (ladder + denominator * t) / (denominator + level_shift)
         ret[reach, j] = new.astype(jnp.bfloat16)
         for d in shifts:
             pl.when(feasible(pos + d, pos, j))(lambda j=j, d=d: give_back(j, d).start())
 
+    last = vectors - 1
+    for j in range(WORK):
+        across(j, 0, 0).wait_recv()
+        for h in range(1, nz):
+            for way in range(2):
+                pl.when(arrives(h - 1, way))(lambda j=j, h=h, way=way: across(j, h, way).wait_recv())
+    sent = 0
     for q in range(vectors):
-        t = q + ahead + 1
-        if q > 0 and t < groups:
-            group(t)
+        while sent < min(vectors, q + 3):
+            group(lead * (steps - 1) + sent)
+            sent += 1
+        near_first(q)
+        for j in range(WORK):
+            near_second(q, j)
+            if q == last:
+                share(0, j)
+    for q in range(vectors):
         for way in range(2):
             ring(steps - 1, q, way).wait_recv()
         for j in range(WORK):
-            if q == 0:
-                across(j, 0, 0).wait_recv()
-                for h in range(1, nz):
-                    for way in range(2):
-                        pl.when(arrives(h - 1, way))(lambda j=j, h=h, way=way: across(j, h, way).wait_recv())
-            pair_first(q, j)
-            if q == vectors - 1 and j > 0:
-                spread(j - 1)
-            pair_second(q, j)
-            if q == vectors - 1:
-                share(j)
-    for j in range(WORK - 1):
-        chain(j, go_on)
-    spread(WORK - 1)
-    for j in range(WORK - 1):
+            far(q, j)
+            if q == last:
+                share(1, j)
+                share(2, j)
+        if q == 0:
+            for j in range(WORK):
+                chain(0, j, True)
+        elif q == 1:
+            chain(0, 0, False)
+        elif q == 2:
+            chain(0, 1, False)
+    for j in range(WORK):
+        for kind in (1, 2):
+            chain(kind, j, True)
+    for j in range(WORK):
+        for kind in (1, 2):
+            chain(kind, j, False)
         finish(j)
-    chain(WORK - 1, go_on)
-    finish(WORK - 1)
     for j in range(WORK):
         for d in shifts:
             pl.when(feasible(pos, pos + d, j))(lambda j=j, d=d: give_back(j, -d).wait_recv())
@@ -342,8 +388,9 @@
                 pl.when(leaves(h, way))(lambda j=j, h=h, way=way: along(j, h, way).wait_send())
                 pl.when(arrives(h, way))(lambda j=j, h=h, way=way: across(j, h + 1, way).wait_send())
         for k in range(nz):
-            pl.when(z != k)(lambda j=j, k=k: incoming(j, k).wait_send())
-        to_sibling(j).wait_send()
+            for w in range(2):
+                pl.when(z != k)(lambda j=j, k=k, w=w: incoming(w, j, k).wait_send())
+                to_sibling(w, j, k).wait_send()
     for q in range(vectors):
         for step in range(steps):
             for way in range(2):
@@ -358,6 +405,7 @@
         vectors, block, _ = factors.shape
         reach = reach_of(n, slots)
         span, nz, steps = 2 * reach + 1, m // 2, n // 2
+        near = (n - 1) * block
         bf16, f32 = jnp.bfloat16, jnp.float32
         dma = pltpu.SemaphoreType.DMA
         vmem, smem = pl.BlockSpec(memory_space=pltpu.VMEM), pl.BlockSpec(memory_space=pltpu.SMEM)
@@ -370,21 +418,28 @@
             scratch_shapes=[
                 pltpu.VMEM((vectors, n, block, size), bf16),
                 pltpu.VMEM((WORK, m, rows, size), bf16),
-                pltpu.VMEM((size, size), bf16),
-                pltpu.VMEM((WORK, size, size), f32),
+                pltpu.VMEM((vectors, WORK, size, near), bf16),
+                pltpu.VMEM((size, block), bf16),
+                pltpu.VMEM((WORK, size, near), f32),
+                pltpu.VMEM((WORK, size, block), f32),
                 pltpu.VMEM((span, WORK, rows, size), bf16),
                 pltpu.VMEM((span, WORK, rows, size), bf16),
-                pltpu.VMEM((WORK, nz, rows, size), bf16),
-                pltpu.VMEM((WORK, nz, rows, size), bf16),
-                pltpu.VMEM((WORK, nz, rows, size), bf16),
-                pltpu.VMEM((WORK, nz + 1, rows, size), bf16),
+                pltpu.VMEM((WORK, nz, rows, near), bf16),
+                pltpu.VMEM((WORK, nz, rows, block), bf16),
+                pltpu.VMEM((WORK, nz, rows, near), bf16),
+                pltpu.VMEM((WORK, nz, rows, block), bf16),
+                pltpu.VMEM((WORK, nz, rows, near), bf16),
+                pltpu.VMEM((WORK, nz, rows, block), bf16),
+                pltpu.VMEM((WORK, nz + 1, rows, near), bf16),
+                pltpu.VMEM((WORK, nz + 1, rows, block), bf16),
+                pltpu.VMEM((rows, size), f32),
                 pltpu.VMEM((span, WORK, rows, size), bf16),
                 dma((2, steps, vectors)), dma((2, steps, vectors)),
                 dma((span, WORK)), dma((span, WORK)),
                 dma((WORK, 2, nz)), dma((WORK, 2, nz)),
                 dma((WORK, 2, nz)), dma((WORK, 2, nz)),
-                dma((WORK,)), dma((WORK,)),
-                dma((WORK, nz)), dma((WORK, nz + 1)),
+                dma((2, WORK, nz)), dma((2, WORK, nz)),
+                dma((2, WORK, nz)), dma((2, WORK, nz + 1)),
                 dma((span, WORK)), dma((span, WORK)),
             ],
             cost_estimate=pl.CostEstimate(flops=flops, bytes_accessed=2 * vectors * size * size, transcendentals=0),

time: 95.4 us -> 102 us (1.069)
  the two profiles are of different devices: /device:TPU:0 before, /device:TPU:26 now
where the time goes in v5:
time: 102 us
  Pallas kernels  100 us (98%)
  local copies, waits for them, and re-layouts  1.92 us (2%)
    pallas_call x1, Pallas kernels, per_device(): pl.pallas_call(functools.partial(kernel, n, m, reach), out_shape=jax.Shap...  100 us

profile of v5, /device:TPU:26, one launch (start us, length us, event | category | flops | bytes accessed | tf_op | source)
XLA Modules:
  0.0 101.9 jit_solution(805337056156421290)
XLA Ops:
  0.0 100.0 %shard_map.64 = bf16[4,96,768]{2,1,0:T(8,128)(2,1)} custom-call(bf16[4,96,768]{2,1,0:T(8,128)(2,1)} %amps.1, bf16[4,192,768]{2,1,0:T(8,128)(2,1)} %factors.1, s32[4]{0:T(128)} %counts.1, s32[2,16]{1,0:T(2,128)} %bitcast.1, f32[24]{0:T(128)} %occ.1, f32[768]{0:T(1024)} %vir.1), custom_call_target="tpu_custom_call" | custom-call | flops 14495514624 | bytes 4718592 | tf_op jit(solution)/shard_map/pallas_call | solution.py:413
  100.0 1.9 %copy.8 = bf16[4,96,768]{2,1,0:T(8,128)(2,1)} copy(bf16[4,96,768]{2,1,0:T(8,128)(2,1)} %shard_map.64) | data formatting | bytes 1179648

commit v6 on v3

--- a/solution.py
+++ b/solution.py
@@ -221,51 +221,22 @@
     def to_sibling(j):
         return remote(sib_out.at[j], sib_in.at[j], b_send.at[j], b_recv.at[j], col=sibling)
 
-    def onward(j, k, way):
-        target = (jnp.minimum(z + 1, nz - 1) if way == 0 else jnp.maximum(z - 1, 0)) * 2 + core
-        slot = k if way == 0 else jnp.where(k == z - 1, nz, k)
-        return remote(z_out.at[j, k], z_in.at[j, slot], z_send.at[j, k], z_recv.at[j, slot], col=target)
-
-    def incoming(j, slot):
-        sent = min(slot, nz - 1) if isinstance(slot, int) else slot
-        return remote(z_out.at[j, sent], z_in.at[j, slot], z_send.at[j, sent], z_recv.at[j, slot], col=sibling)
+    def to_owner(j, o):
+        return remote(z_out.at[j, o], z_in.at[j, o], z_send.at[j, o], z_recv.at[j, o],
+                      col=((z + o) % nz) * 2 + core)
 
     def share(j):
         for k in range(nz):
             sib_out[j, k] = acc[j, rows_of(2 * k + 1 - core), :].astype(jnp.bfloat16)
         to_sibling(j).start()
 
-    def chain(j, action):
-        def one_way(way):
-            for i in range(nz - 1):
-                k = nz - 1 - i if way == 0 else i
-                ahead_of = (k > z) if way == 0 else (k < z)
-                first = (z == 0) if way == 0 else (z == nz - 1)
-                action(j, k, way, ahead_of, first)
-
-        low = z < nz // 2
-        pl.when(low)(lambda: one_way(0))
-        one_way(1)
-        pl.when(jnp.logical_not(low))(lambda: one_way(0))
-
-    def begin(j, k, way, ahead_of, first):
-        @pl.when(ahead_of & first)
-        def _():
-            total = acc[j, rows_of(2 * k + core), :] + sib_in[j, k].astype(jnp.float32)
-            z_out[j, k] = total.astype(jnp.bfloat16)
-            onward(j, k, way).start()
-
-    def go_on(j, k, way, ahead_of, first):
-        @pl.when(ahead_of & jnp.logical_not(first))
-        def _():
-            total = acc[j, rows_of(2 * k + core), :] + sib_in[j, k].astype(jnp.float32)
-            incoming(j, k).wait_recv()
-            z_out[j, k] = (total + z_in[j, k].astype(jnp.float32)).astype(jnp.bfloat16)
-            onward(j, k, way).start()
-
     def spread(j):
         to_sibling(j).wait_recv()
-        chain(j, begin)
+        for o in range(1, nz):
+            k = (z + o) % nz
+            total = acc[j, rows_of(2 * k + core), :] + sib_in[j, k].astype(jnp.float32)
+            z_out[j, o] = total.astype(jnp.bfloat16)
+            to_owner(j, o).start()
 
     def finish(j):
         rank = pos * WORK + j
@@ -278,20 +249,10 @@
         levels = jnp.broadcast_to(vir[...], (rows, size))
         mine = jnp.sum(jnp.where(here == there, levels, 0.0), axis=1, keepdims=True)
         denominator = mine + levels - energy
-        own = rows_of(col)
-        acc[j, own, :] += sib_in[j, z].astype(jnp.float32)
-
-        @pl.when(z > 0)
-        def _():
-            incoming(j, z).wait_recv()
-            acc[j, own, :] += z_in[j, z].astype(jnp.float32)
-
-        @pl.when(z < nz - 1)
-        def _():
-            incoming(j, nz).wait_recv()
-            acc[j, own, :] += z_in[j, nz].astype(jnp.float32)
-
-        ladder = acc[j, own, :]
+        ladder = acc[j, rows_of(col), :] + sib_in[j, z].astype(jnp.float32)
+        for o in range(1, nz):
+            to_owner(j, o).wait_recv()
+            ladder = ladder + z_in[j, o].astype(jnp.float32)
         t = held[j, col].astype(jnp.float32)
         new = t - (ladder + denominator * t) / (denominator + level_shift)
         ret[reach, j] = new.astype(jnp.bfloat16)
@@ -316,13 +277,9 @@
             pair_second(q, j)
             if q == vectors - 1:
                 share(j)
-    for j in range(WORK - 1):
-        chain(j, go_on)
     spread(WORK - 1)
-    for j in range(WORK - 1):
+    for j in range(WORK):
         finish(j)
-    chain(WORK - 1, go_on)
-    finish(WORK - 1)
     for j in range(WORK):
         for d in shifts:
             pl.when(feasible(pos, pos + d, j))(lambda j=j, d=d: give_back(j, -d).wait_recv())
@@ -341,8 +298,8 @@
             for h in range(nz - 1):
                 pl.when(leaves(h, way))(lambda j=j, h=h, way=way: along(j, h, way).wait_send())
                 pl.when(arrives(h, way))(lambda j=j, h=h, way=way: across(j, h + 1, way).wait_send())
-        for k in range(nz):
-            pl.when(z != k)(lambda j=j, k=k: incoming(j, k).wait_send())
+        for o in range(1, nz):
+            to_owner(j, o).wait_send()
         to_sibling(j).wait_send()
     for q in range(vectors):
         for step in range(steps):

time: 95.4 us -> 96.9 us (1.016)
  no operation moved by 1% of the time
where the time goes in v6:
time: 96.9 us; the launch traced here: 96.1 us
  Pallas kernels  94.1 us (97%)
  local copies, waits for them, and re-layouts  1.92 us (2%)
    pallas_call x1, Pallas kernels, per_device(): pl.pallas_call(functools.partial(kernel, n, m, reach), out_shape=jax.Shap...  94.1 us

profile of v6, /device:TPU:0, one launch (start us, length us, event | category | flops | bytes accessed | tf_op | source)
XLA Modules:
  0.0 96.1 jit_solution(15552211387951501345)
XLA Ops:
  0.0 94.1 %shard_map.64 = bf16[4,96,768]{2,1,0:T(8,128)(2,1)} custom-call(bf16[4,96,768]{2,1,0:T(8,128)(2,1)} %amps.1, bf16[4,192,768]{2,1,0:T(8,128)(2,1)} %factors.1, s32[4]{0:T(128)} %counts.1, s32[2,16]{1,0:T(2,128)} %bitcast.1, f32[24]{0:T(128)} %occ.1, f32[768]{0:T(1024)} %vir.1), custom_call_target="tpu_custom_call" | custom-call | flops 14495514624 | bytes 4718592 | tf_op jit(solution)/shard_map/pallas_call | solution.py:322
  94.1 1.9 %copy.8 = bf16[4,96,768]{2,1,0:T(8,128)(2,1)} copy(bf16[4,96,768]{2,1,0:T(8,128)(2,1)} %shard_map.64) | data formatting | bytes 1179648

commit v7 on v3

--- a/solution.py
+++ b/solution.py
@@ -107,7 +107,7 @@
 
     steps = n // 2
     part = block // 2
-    lead = 3
+    lead = 2
 
     def ring(step, q, way):
         move = 1 if way == 0 else -1
@@ -140,32 +140,14 @@
 
     lax.fori_loop(0, vectors, own_block, 0)
 
-    def passed(h, way):
-        return z - h if way == 0 else z + h
-
-    def arrives(h, way):
-        return passed(h + 1, way) >= 0 if way == 0 else passed(h + 1, way) < nz
-
-    def leaves(h, way):
-        there = passed(h, way) >= 0 if way == 0 else passed(h, way) < nz
-        return there & (z + 1 < nz if way == 0 else z > 0)
-
-    def along(j, h, way):
-        src = passed(h, way) * 2 + core
-        target = (jnp.minimum(z + 1, nz - 1) if way == 0 else jnp.maximum(z - 1, 0)) * 2 + core
-        return remote(held.at[j, src], held.at[j, src], t_send.at[j, way, h], t_recv.at[j, way, h], col=target)
-
-    def across(j, h, way):
-        src = passed(h, way) * 2 + core
-        return remote(held.at[j, src], held.at[j, src], f_send.at[j, way, h], f_recv.at[j, way, h], col=sibling)
-
-    def hop(j, h, way):
-        @pl.when(arrives(h - 1, way))
-        def _():
-            along(j, h - 1, way).wait_recv()
-            if h < nz - 1:
-                pl.when(leaves(h, way))(lambda: along(j, h, way).start())
-            across(j, h, way).start()
+    def along(j, o):
+        return remote(held.at[j, col], held.at[j, col], t_send.at[j, o], t_recv.at[j, o],
+                      col=((z + o) % nz) * 2 + core)
+
+    def across(j, o):
+        from_z = (z - o + nz) % nz
+        src = from_z * 2 + core
+        return remote(held.at[j, src], held.at[j, src], f_send.at[j, o], f_recv.at[j, o], col=sibling)
 
     for j in range(WORK):
         for d in shifts:
@@ -175,19 +157,18 @@
         for d in shifts:
             chosen = jnp.where(src == d, shuf[d + reach, j], chosen)
         held[j, col] = chosen
-        for way in range(2):
-            pl.when(leaves(0, way))(lambda j=j, way=way: along(j, 0, way).start())
-        across(j, 0, 0).start()
-
-    later = list(range(lead, min(ahead + 2, groups)))
-    for h in range(1, nz):
-        for j in range(WORK):
-            for way in range(2):
-                hop(j, h, way)
-        if later and h > 1:
-            group(later.pop(0))
-    for t in later:
+        for o in range(1, nz):
+            along(j, o).start()
+        across(j, 0).start()
+
+    for t in range(2, min(ahead + 1, groups)):
         group(t)
+    for j in range(WORK):
+        for o in range(1, nz):
+            along(j, o).wait_recv()
+            across(j, o).start()
+    if ahead + 1 < groups:
+        group(ahead + 1)
 
     tile = size // 2
 
@@ -306,10 +287,8 @@
             ring(steps - 1, q, way).wait_recv()
         for j in range(WORK):
             if q == 0:
-                across(j, 0, 0).wait_recv()
-                for h in range(1, nz):
-                    for way in range(2):
-                        pl.when(arrives(h - 1, way))(lambda j=j, h=h, way=way: across(j, h, way).wait_recv())
+                for o in range(nz):
+                    across(j, o).wait_recv()
             pair_first(q, j)
             if q == vectors - 1 and j > 0:
                 spread(j - 1)
@@ -336,11 +315,10 @@
         for d in shifts:
             pl.when(feasible(pos, pos + d, j))(lambda j=j, d=d: shuffle(j, d).wait_send())
             pl.when(feasible(pos + d, pos, j))(lambda j=j, d=d: give_back(j, d).wait_send())
-        across(j, 0, 0).wait_send()
-        for way in range(2):
-            for h in range(nz - 1):
-                pl.when(leaves(h, way))(lambda j=j, h=h, way=way: along(j, h, way).wait_send())
-                pl.when(arrives(h, way))(lambda j=j, h=h, way=way: across(j, h + 1, way).wait_send())
+        for o in range(1, nz):
+            along(j, o).wait_send()
+        for o in range(nz):
+            across(j, o).wait_send()
         for k in range(nz):
             pl.when(z != k)(lambda j=j, k=k: incoming(j, k).wait_send())
         to_sibling(j).wait_send()
@@ -381,8 +359,8 @@
                 pltpu.VMEM((span, WORK, rows, size), bf16),
                 dma((2, steps, vectors)), dma((2, steps, vectors)),
                 dma((span, WORK)), dma((span, WORK)),
-                dma((WORK, 2, nz)), dma((WORK, 2, nz)),
-                dma((WORK, 2, nz)), dma((WORK, 2, nz)),
+                dma((WORK, nz)), dma((WORK, nz)),
+                dma((WORK, nz)), dma((WORK, nz)),
                 dma((WORK,)), dma((WORK,)),
                 dma((WORK, nz)), dma((WORK, nz + 1)),
                 dma((span, WORK)), dma((span, WORK)),

time: 95.4 us -> 95.6 us (level)
  no operation moved by 1% of the time
where the time goes in v7:
time: 95.6 us; the launch traced here: 95.4 us
  Pallas kernels  93.5 us (98%)
  local copies, waits for them, and re-layouts  1.92 us (2%)
    pallas_call x1, Pallas kernels, per_device(): pl.pallas_call(functools.partial(kernel, n, m, reach), out_shape=jax.Shap...  93.5 us
    unnamed x1, local copies, waits for them, and re-layouts  1.92 us

profile of v7, /device:TPU:0, one launch (start us, length us, event | category | flops | bytes accessed | tf_op | source)
XLA Modules:
  0.0 95.4 jit_solution(3552900759379187824)
XLA Ops:
  0.0 93.5 %shard_map.64 = bf16[4,96,768]{2,1,0:T(8,128)(2,1)} custom-call(bf16[4,96,768]{2,1,0:T(8,128)(2,1)} %amps.1, bf16[4,192,768]{2,1,0:T(8,128)(2,1)} %factors.1, s32[4]{0:T(128)} %counts.1, s32[2,16]{1,0:T(2,128)} %bitcast.1, f32[24]{0:T(128)} %occ.1, f32[768]{0:T(1024)} %vir.1), custom_call_target="tpu_custom_call" | custom-call | flops 14495514624 | bytes 4718592 | tf_op jit(solution)/shard_map/pallas_call | solution.py:343
  93.5 1.9 %copy.8 = bf16[4,96,768]{2,1,0:T(8,128)(2,1)} copy(bf16[4,96,768]{2,1,0:T(8,128)(2,1)} %shard_map.64) | data formatting | bytes 1179648
